TPU v7x, 256 devices: a whole 4x4x8 slice. The times are simulated.
256 devices in a mesh: row: 16 (over x, z_hi, core), col: 16 (over z_lo, y).
Axes of the slice: x: 4, y: 4, z: 8 (z_hi: 2, z_lo: 4; z = z_hi * 4 + z_lo), core: 2. Of those that a mesh axis runs over, the one named last changes fastest.
Arguments:
- inputs: bfloat16 [512, 12288], P('col', 'row'), may hold values from -6 to 6
- w_up: bfloat16 [12288, 24576], P('row', 'col'), may hold values from -0.0546875 to 0.0546875
- w_down: bfloat16 [24576, 12288], P('col', 'row'), may hold values from -0.0390625 to 0.0390625
- grad_out: bfloat16 [512, 12288], P('col', 'row'), may hold values from -1.5 to 1.5
Outputs:
- outputs: bfloat16 [512, 12288], P('col', 'row')
- grad_in: bfloat16 [512, 12288], P('col', 'row')
- grad_up: bfloat16 [12288, 24576], P('row', 'col')
- grad_down: bfloat16 [24576, 12288], P('col', 'row')
All inputs are finite; a program needn't handle non-finite values.
Results may differ from a plain program's by a relative error of at most 0.005.
Values may be sent and summed in bfloat16 or wider, within the bound.
A program may use at most 64 MiB of HBM per device.

v0:
```python
import jax
import jax.numpy as jnp
from jax import lax
from jax.sharding import PartitionSpec as P


def gelu_tanh(value):
    inner = 0.7978845608 * (value + 0.044715 * value * value * value)
    return 0.5 * value * (1.0 + jnp.tanh(inner))


def activate(hidden, grad_active):
    active, pullback = jax.vjp(gelu_tanh, hidden)
    return (active.astype(jnp.bfloat16), pullback(grad_active)[0].astype(jnp.bfloat16))


def contract(left, right, left_dim, right_dim):
    return lax.dot_general(
        left, right, (((left_dim,), (right_dim,)), ((), ())), preferred_element_type=jnp.float32
    )


def on_device(inputs, w_up, w_down, grad_out):
    all_inputs, all_grads = (
        lax.all_gather(inputs, "col", axis=0, tiled=True),
        lax.all_gather(grad_out, "col", axis=0, tiled=True),
    )
    part_hidden = jnp.dot(all_inputs, w_up, preferred_element_type=jnp.float32)
    part_active = contract(all_grads, w_down, 1, 1)
    hidden, grad_active = (
        lax.psum_scatter(part_hidden, "row", scatter_dimension=0, tiled=True),
        lax.psum_scatter(part_active, "row", scatter_dimension=0, tiled=True),
    )
    active, grad_hidden = activate(hidden, grad_active)
    all_active, all_hidden = (
        lax.all_gather(active, "row", axis=0, tiled=True),
        lax.all_gather(grad_hidden, "row", axis=0, tiled=True),
    )
    grad_down = contract(all_active, all_grads, 0, 0).astype(jnp.bfloat16)
    grad_up = contract(all_inputs, all_hidden, 0, 0).astype(jnp.bfloat16)
    part_output = jnp.dot(all_active, w_down, preferred_element_type=jnp.float32)
    part_input = contract(all_hidden, w_up, 1, 1)
    outputs, grad_in = (
        lax.psum_scatter(part_output, "col", scatter_dimension=0, tiled=True),
        lax.psum_scatter(part_input, "col", scatter_dimension=0, tiled=True),
    )
    return (outputs.astype(jnp.bfloat16), grad_in.astype(jnp.bfloat16), grad_up, grad_down)


def solution(mesh):
    placed = (P("col", "row"), P("row", "col"), P("col", "row"), P("col", "row"))
    return jax.shard_map(
        on_device,
        mesh=mesh,
        in_specs=placed,
        out_specs=(P("col", "row"), P("col", "row"), P("row", "col"), P("col", "row")),
        check_vma=False,
    )
```

profile of v0, /device:TPU:1, one launch (start us, length us, event | category | flops | bytes accessed | tf_op | source)
XLA Modules:
  0.0 535.4 jit_solution(13088520077350493778)
XLA Ops:
  7.2 0.0 copy-start
  7.2 0.0 reduce-scatter.5.cloned.1.call-start
  7.2 42.6 %all_gather.12 = bf16[512,768]{1,0:T(8,128)(2,1)S(1)} all-gather(bf16[32,768]{1,0:T(8,128)(2,1)} %param.4), channel_id=1, replica_groups=mesh['row'=16,'col'=16] {'col'}, dimensions={0}, use_global_device_ids=true | all-gather | bytes 835584 | tf_op jit(solution)/shard_map/all_gather | solution.py:25
  49.8 4.7 fusion.9
  54.5 0.0 copy-start.3
  54.5 0.0 reduce-scatter.5.cloned.1.call-update
  54.6 0.0 reduce-scatter.9.cloned.1.call-start
  54.6 0.7 copy-done.3
  55.3 35.0 %all_gather.14 = bf16[512,768]{1,0:T(8,128)(2,1)S(1)} all-gather(bf16[32,768]{1,0:T(8,128)(2,1)S(1)} %copy-done.3), channel_id=1, replica_groups=mesh['row'=16,'col'=16] {'col'}, dimensions={0}, use_global_device_ids=true | all-gather | bytes 835584 | tf_op jit(solution)/shard_map/all_gather | solution.py:26
  90.3 0.0 copy-start.1
  90.3 0.9 copy-done.1
  91.2 0.0 copy-done
  91.2 3.1 fusion.11
  94.3 0.0 reduce-scatter.9.cloned.1.call-update
  94.3 0.0 all-gather.3.cloned.1.call-start
  94.4 59.1 %reduce-scatter.5.cloned.1.call-done = f32[32,1536]{1,0:T(8,128)} async-done(((f32[512,1536]{1,0:T(8,128)}), f32[32,1536]{1,0:T(8,128)}) %reduce-scatter.5.cloned.1.call-update) | async-done | bytes 196624 | tf_op jit(solution)/shard_map/reduce_scatter | solution.py:31
  153.4 95.9 %reduce-scatter.9.cloned.1.call-done = f32[32,1536]{1,0:T(8,128)} async-done(((f32[512,1536]{1,0:T(8,128)}), f32[32,1536]{1,0:T(8,128)}) %reduce-scatter.9.cloned.1.call-update) | async-done | bytes 196624 | tf_op jit(solution)/shard_map/reduce_scatter | solution.py:32
  249.3 1.9 fusion.5
  251.2 0.0 all-gather.3.cloned.1.call-update
  251.2 0.0 all-gather.5.cloned.1.call-start
  251.2 0.5 all-gather.5.cloned.1.call-update
  251.8 0.0 reduce-scatter.7.cloned.1.call-start
  251.8 58.0 %all-gather.3.cloned.1.call-done = bf16[512,1536]{1,0:T(8,128)(2,1)} async-done(((bf16[32,1536]{1,0:T(8,128)(2,1)}), bf16[512,1536]{1,0:T(8,128)(2,1)}) %all-gather.3.cloned.1.call-update) | async-done | bytes 1572880 | tf_op jit(solution)/shard_map/all_gather | solution.py:36
  309.8 3.9 fusion.10
  313.7 0.0 reduce-scatter.7.cloned.1.call-update
  313.8 0.0 reduce-scatter.11.cloned.1.call-start
  313.8 54.3 %all-gather.5.cloned.1.call-done = bf16[512,1536]{1,0:T(8,128)(2,1)} async-done(((bf16[32,1536]{1,0:T(8,128)(2,1)}), bf16[512,1536]{1,0:T(8,128)(2,1)}) %all-gather.5.cloned.1.call-update) | async-done | bytes 1572880 | tf_op jit(solution)/shard_map/all_gather | solution.py:37
  368.1 4.7 fusion.12
  372.8 0.0 reduce-scatter.11.cloned.1.call-update
  372.8 4.2 fusion
  377.1 0.0 copy-start.2
  377.1 4.3 copy.8
  381.4 0.0 copy-done.2
  381.4 4.2 convolution_convert_fusion
  385.7 55.8 %reduce-scatter.7.cloned.1.call-done = f32[32,768]{1,0:T(8,128)} async-done(((f32[512,768]{1,0:T(8,128)}), f32[32,768]{1,0:T(8,128)}) %reduce-scatter.7.cloned.1.call-update) | async-done | bytes 98320 | tf_op jit(solution)/shard_map/reduce_scatter | solution.py:44
  441.5 1.5 convert_element_type.22
  443.0 84.0 %reduce-scatter.11.cloned.1.call-done = f32[32,768]{1,0:T(8,128)} async-done(((f32[512,768]{1,0:T(8,128)}), f32[32,768]{1,0:T(8,128)}) %reduce-scatter.11.cloned.1.call-update) | async-done | bytes 98320 | tf_op jit(solution)/shard_map/reduce_scatter | solution.py:45
  527.0 1.5 convert_element_type.24
Async XLA Ops:
  7.2 84.0 %copy-start = (bf16[1536,768]{1,0:T(8,128)(2,1)S(1)}, bf16[1536,768]{1,0:T(8,128)(2,1)}, u32[]{:S(2)}) copy-start(bf16[1536,768]{1,0:T(8,128)(2,1)} %param.6) | copy-start | bytes 7077892
  7.2 146.3 %reduce-scatter.5.cloned.1.call-start = ((), (), s32[]{:S(2)}) async-start(), calls=%async_computation.4 | async-start | bytes 3342336 | tf_op jit(solution)/shard_map/reduce_scatter | solution.py:31
  54.5 0.8 copy-start.3
  54.6 194.8 %reduce-scatter.9.cloned.1.call-start = ((), (), s32[]{:S(2)}) async-start(), calls=%async_computation.7 | async-start | bytes 3342336 | tf_op jit(solution)/shard_map/reduce_scatter | solution.py:32
  90.3 0.9 copy-start.1
  94.3 215.4 %all-gather.3.cloned.1.call-start = ((), (), s32[]{:S(2)}) async-start(), calls=%async_computation.5 | async-start | bytes 1671168 | tf_op jit(solution)/shard_map/all_gather | solution.py:36
  251.2 116.9 %all-gather.5.cloned.1.call-start = ((), (), s32[]{:S(2)}) async-start(), calls=%async_computation.8 | async-start | bytes 1671168 | tf_op jit(solution)/shard_map/all_gather | solution.py:37
  251.8 189.7 %reduce-scatter.7.cloned.1.call-start = ((), (), s32[]{:S(2)}) async-start(), calls=%async_computation.6 | async-start | bytes 1671168 | tf_op jit(solution)/shard_map/reduce_scatter | solution.py:44
  313.8 213.3 %reduce-scatter.11.cloned.1.call-start = ((), (), s32[]{:S(2)}) async-start(), calls=%async_computation.9 | async-start | bytes 1671168 | tf_op jit(solution)/shard_map/reduce_scatter | solution.py:45
  377.1 4.4 copy-start.2
Sparse Core Ops, SparseCore 0:
  54.7 98.7 reduce-scatter.4
  157.7 91.5 reduce-scatter.8
  252.6 57.1 all-gather.2
  312.9 55.1 all-gather.4
  370.5 70.9 reduce-scatter.6
  444.0 82.9 reduce-scatter.10
where the time goes:
time: 546 us; the launch traced here: 535 us
  waiting for transfers between devices  408 us (75%)
  blocking collectives  77.6 us (14%)
  matrix products  24.9 us (5%)
  between operations  14.1 us (3%)
  local copies, waits for them, and re-layouts  5.99 us (1%)
    reduce_scatter x1, waiting for transfers between devices, on_device(): lax.psum_scatter(part_active, 'row', scatter_dimension=0, tiled=True)  95.9 us
    reduce_scatter x1, waiting for transfers between devices, on_device(): lax.psum_scatter(part_input, 'col', scatter_dimension=0, tiled=True)  84 us
    reduce_scatter x1, waiting for transfers between devices, on_device(): lax.psum_scatter(part_hidden, 'row', scatter_dimension=0, tiled=True)  59.1 us
    all_gather x1, waiting for transfers between devices, on_device(): lax.all_gather(active, 'row', axis=0, tiled=True)  58 us
    reduce_scatter x1, waiting for transfers between devices, on_device(): lax.psum_scatter(part_output, 'col', scatter_dimension=0, tiled=True)  55.8 us
    all_gather x1, waiting for transfers between devices, on_device(): lax.all_gather(grad_hidden, 'row', axis=0, tiled=True)  54.3 us
    all_gather x1, blocking collectives, on_device(): lax.all_gather(inputs, 'col', axis=0, tiled=True)  42.6 us
    all_gather x1, blocking collectives, on_device(): lax.all_gather(grad_out, 'col', axis=0, tiled=True)  35 us
  transfers between devices with their start and end apart: 6, of which 6 were waited for; matrix products, arithmetic and copies ran while one was open for 5% of the time, Pallas kernels for 0%

commit v1 on v0

v1 whole, which is shorter than its diff:
```python
import functools

import jax
import jax.numpy as jnp
from jax import lax
from jax.experimental import pallas as pl
from jax.experimental.pallas import tpu as pltpu
from jax.sharding import PartitionSpec as P

MESH = pl.DeviceIdType.MESH
BF16, F32 = jnp.bfloat16, jnp.float32
ORDER = (
    (0, 1, 0), (1, 0, 0), (0, 1, 1), (1, 0, 1), (2, 0, 0), (0, 2, 0), (0, 2, 1), (1, 1, 0),
    (2, 0, 1), (0, 3, 0), (1, 1, 1), (2, 1, 0), (0, 3, 1), (3, 0, 0), (1, 2, 0), (2, 1, 1),
    (1, 2, 1), (3, 0, 1), (2, 2, 0), (1, 3, 0), (3, 1, 0), (2, 2, 1), (4, 0, 0), (1, 3, 1),
    (3, 1, 1), (2, 3, 0), (4, 0, 1), (3, 2, 0), (2, 3, 1), (4, 1, 0), (3, 2, 1), (5, 0, 0),
    (4, 1, 1), (3, 3, 0), (5, 0, 1), (3, 3, 1), (4, 2, 0), (5, 1, 0), (6, 0, 0), (4, 2, 1),
    (5, 1, 1), (7, 0, 0), (6, 0, 1), (4, 3, 0), (4, 3, 1), (6, 1, 0), (5, 2, 0), (7, 0, 1),
    (5, 2, 1), (7, 1, 0), (6, 1, 1), (8, 0, 0), (5, 3, 0), (7, 1, 1), (6, 2, 0), (5, 3, 1),
    (8, 0, 1), (6, 2, 1), (7, 2, 0), (8, 1, 0), (7, 2, 1), (6, 3, 0), (8, 1, 1), (6, 3, 1),
    (7, 3, 0), (7, 3, 1), (8, 2, 0), (8, 2, 1), (8, 3, 0), (8, 3, 1),
)


def tanh_of(value):
    return jnp.tanh(0.7978845608 * (value + 0.044715 * value * value * value))


def gelu(value):
    return 0.5 * value * (1.0 + tanh_of(value))


def gelu_slope(value):
    t = tanh_of(value)
    inner_slope = 0.7978845608 * (1.0 + 3.0 * 0.044715 * value * value)
    return 0.5 * (1.0 + t) + 0.5 * value * (1.0 - t * t) * inner_slope


def contract(left, right, left_dim, right_dim):
    return lax.dot_general(
        left, right, (((left_dim,), (right_dim,)), ((), ())), preferred_element_type=F32
    )


def at(start, size):
    return pl.ds(pl.multiple_of(start, size), size)


def kernel(
    inputs, w_up, w_down, grad_out, outputs, grad_in, grad_up, grad_down,
    tokens, up, down, act, up_out, down_out,
    core_out, core_in, mine, x_out, x_in, sums, zh_out, zh_in, hidden,
    part, y_out, y_in, kept, z_out, z_in,
    load_sem, store_sem, own_sem, sent, got,
):
    row, col = lax.axis_index("row"), lax.axis_index("col")
    x, zh, core = row // 4, (row // 2) % 2, row % 2
    zl, y = col // 4, col % 4
    other_core = (row + 1 - 2 * core, col)
    partner = (row + 2 - 4 * zh, col)
    xs = [((row + 4 * d) % 16, col) for d in (1, 2, 3)]
    ys = [(row, zl * 4 + (y + d) % 4) for d in (1, 2, 3)]
    planes = [zl, zl + 1 - 2 * (zl % 2), (zl + 2) % 4, 3 - zl]
    zs = [(row, plane * 4 + y) for plane in planes[1:]]
    shards = (inputs, grad_out)

    loads = []
    for half in range(2):
        for k, (src, dst) in enumerate((
            (w_up.at[:, pl.ds(half * 768, 768)], up.at[half]),
            (w_down.at[pl.ds(half * 768, 768)], down.at[half]),
        )):
            loads.append(pltpu.make_async_copy(src, dst, load_sem.at[k, half]))
    own = [
        pltpu.make_async_copy(shards[a], tokens.at[a, at(y * 32, 32)], own_sem.at[a])
        for a in range(2)
    ]
    for copy in own + loads:
        copy.start()

    barrier = pltpu.get_barrier_semaphore()
    everyone = [other_core, partner] + xs + ys + zs
    for device in everyone:
        pl.semaphore_signal(barrier, inc=1, device_id=device, device_id_type=MESH)
    pl.semaphore_wait(barrier, len(everyone))

    flights = {}

    def send(src, dst, device, send_sem, recv_sem, rows):
        pltpu.make_async_remote_copy(
            src_ref=src, dst_ref=dst, send_sem=sent.at[send_sem], recv_sem=got.at[recv_sem],
            device_id=device, device_id_type=MESH,
        ).start()
        flights[send_sem] = flights.get(send_sem, 0) + rows

    def arrived(ref, recv_sem):
        pltpu.make_async_copy(ref, ref, got.at[recv_sem]).wait()

    def sem(step, q):
        return 8 + 8 * step + q

    for a in range(2):
        here = tokens.at[a, at(y * 32, 32)]
        for device in ys:
            send(shards[a], here, device, a, a, 32)
    for j in (1, 2, 3):
        for a in range(2):
            there = tokens.at[a, at(j * 128 + y * 32, 32)]
            send(shards[a], there, zs[j - 1], sem(0, 2 * j + a), sem(0, 2 * j + a), 32)

    weights_here = set()

    def weights(k):
        if k not in weights_here:
            weights_here.add(k)
            for half in range(2):
                loads[2 * half + k].wait()

    for step, j, a in ORDER:
        q = 2 * j + a
        chunk = pl.ds(j * 128, 128)
        group = at(j * 128 + x * 32, 32)
        piece = at(j * 128 + x * 32 + zh * 16, 16)
        if step == 0:
            shard = tokens.at[a, at(j * 128 + y * 32, 32)]
            arrived(shard, sem(0, q))
            for device in ys:
                send(shard, shard, device, q, q, 32)
        elif step == 1:
            if j == 0:
                own[a].wait()
                weights(a)
            arrived(tokens.at[a, pl.ds(j * 128, 96)], q)
            block = tokens[a, chunk]

            def product(half):
                if a == 0:
                    return contract(block, up[half], 1, 0)
                return contract(block, down[half], 1, 1)

            core_out[q] = product(1 - core)
            send(core_out.at[q], core_in.at[q], other_core, sem(1, q), sem(1, q), 256)
            mine[q] = product(core)
        elif step == 2:
            arrived(core_in.at[q], sem(1, q))
            both = mine[q] + core_in[q]
            mine[q] = both
            x_out[q] = both.astype(BF16)
            for d in (1, 2, 3):
                theirs = x_out.at[q, at((x + d) % 4 * 32, 32)]
                send(theirs, x_in.at[q, d - 1], xs[d - 1], sem(2, q), sem(2, q), 32)
        elif step == 3:
            arrived(x_in.at[q], sem(2, q))
            total = mine[q, at(x * 32, 32)]
            for d in range(3):
                total = total + x_in[q, d].astype(F32)
            sums[q] = total
            zh_out[q] = total.astype(BF16)
            send(zh_out.at[q, at((1 - zh) * 16, 16)], zh_in.at[q], partner, sem(3, q), sem(3, q), 16)
        elif step == 4:
            arrived(zh_in.at[q], sem(3, q))
            total = sums[q, at(zh * 16, 16)] + zh_in[q].astype(F32)
            if a == 0:
                hidden[j] = total
                result = gelu(total)
            else:
                result = total * gelu_slope(hidden[j])
            act[a, core, piece] = result.astype(BF16)
            theirs = act.at[a, core, piece]
            send(theirs, theirs, partner, sem(4, q), sem(4, q), 16)
        elif step == 5:
            arrived(zh_in.at[q], sem(4, q))
            theirs = act.at[a, core, group]
            for device in xs:
                send(theirs, theirs, device, sem(5, q), sem(5, q), 32)
        elif step == 6:
            arrived(act.at[a, core, pl.ds(j * 128, 96)], sem(5, q))
            theirs = act.at[a, core, chunk]
            send(theirs, theirs, other_core, sem(6, q), sem(6, q), 128)
        elif step == 7:
            def term(half):
                block = act[a, half, chunk]
                if a == 0:
                    return contract(block, down[half], 1, 0)
                return contract(block, up[half], 1, 1)

            total = term(core)
            arrived(act.at[a, 1 - core, chunk], sem(6, q))
            total = total + term(1 - core)
            part[q] = total
            y_out[q] = total.astype(BF16)
            for d in (1, 2, 3):
                theirs = y_out.at[q, at((y + d) % 4 * 32, 32)]
                send(theirs, y_in.at[q, d - 1], ys[d - 1], sem(7, q), sem(7, q), 32)
        else:
            arrived(y_in.at[q], sem(7, q))
            total = part[q, at(y * 32, 32)]
            for d in range(3):
                total = total + y_in[q, d].astype(F32)
            if j == 0:
                kept[a] = total
            else:
                z_out[a, j - 1] = total.astype(BF16)
                send(z_out.at[a, j - 1], z_in.at[a, j - 1], zs[j - 1], sem(8, a), sem(8, a), 32)
        if (step, j) == (7, 3):
            for half in range(2):
                if a == 0:
                    down_out[half] = contract(act[0, half], tokens[1], 0, 0).astype(BF16)
                    src, dst = down_out.at[half], grad_down.at[pl.ds(half * 768, 768)]
                else:
                    up_out[half] = contract(tokens[0], act[1, half], 0, 0).astype(BF16)
                    src, dst = up_out.at[half], grad_up.at[:, pl.ds(half * 768, 768)]
                pltpu.make_async_copy(src, dst, store_sem.at[a, half]).start()

    for a, result in enumerate((outputs, grad_in)):
        arrived(z_in.at[a], sem(8, a))
        total = kept[a]
        for j in range(3):
            total = total + z_in[a, j].astype(F32)
        result[...] = total.astype(BF16)

    for half in range(2):
        pltpu.make_async_copy(
            down_out.at[half], grad_down.at[pl.ds(half * 768, 768)], store_sem.at[0, half]
        ).wait()
        pltpu.make_async_copy(
            up_out.at[half], grad_up.at[:, pl.ds(half * 768, 768)], store_sem.at[1, half]
        ).wait()
    for send_sem, rows in flights.items():
        ref = tokens.at[0, pl.ds(0, rows)]
        pltpu.make_async_copy(ref, ref, sent.at[send_sem]).wait()


def on_device(inputs, w_up, w_down, grad_out):
    shape = jax.ShapeDtypeStruct
    hbm, vmem = pl.BlockSpec(memory_space=pl.ANY), pl.BlockSpec(memory_space=pltpu.VMEM)
    return pl.pallas_call(
        kernel,
        out_shape=(
            shape((32, 768), BF16), shape((32, 768), BF16),
            shape((768, 1536), BF16), shape((1536, 768), BF16),
        ),
        in_specs=[hbm] * 4,
        out_specs=(vmem, vmem, hbm, hbm),
        scratch_shapes=[
            pltpu.VMEM((2, 512, 768), BF16),
            pltpu.VMEM((2, 768, 768), BF16),
            pltpu.VMEM((2, 768, 768), BF16),
            pltpu.VMEM((2, 2, 512, 768), BF16),
            pltpu.VMEM((2, 768, 768), BF16),
            pltpu.VMEM((2, 768, 768), BF16),
            pltpu.VMEM((8, 128, 768), F32),
            pltpu.VMEM((8, 128, 768), F32),
            pltpu.VMEM((8, 128, 768), F32),
            pltpu.VMEM((8, 128, 768), BF16),
            pltpu.VMEM((8, 3, 32, 768), BF16),
            pltpu.VMEM((8, 32, 768), F32),
            pltpu.VMEM((8, 32, 768), BF16),
            pltpu.VMEM((8, 16, 768), BF16),
            pltpu.VMEM((4, 16, 768), F32),
            pltpu.VMEM((8, 128, 768), F32),
            pltpu.VMEM((8, 128, 768), BF16),
            pltpu.VMEM((8, 3, 32, 768), BF16),
            pltpu.VMEM((2, 32, 768), F32),
            pltpu.VMEM((2, 3, 32, 768), BF16),
            pltpu.VMEM((2, 3, 32, 768), BF16),
            pltpu.SemaphoreType.DMA((2, 2)),
            pltpu.SemaphoreType.DMA((2, 2)),
            pltpu.SemaphoreType.DMA((2,)),
            pltpu.SemaphoreType.DMA((80,)),
            pltpu.SemaphoreType.DMA((80,)),
        ],
        compiler_params=pltpu.CompilerParams(
            collective_id=0, has_side_effects=True, vmem_limit_bytes=56 << 20
        ),
    )(inputs, w_up, w_down, grad_out)


def solution(mesh):
    placed = (P("col", "row"), P("row", "col"), P("col", "row"), P("col", "row"))
    return jax.shard_map(
        on_device,
        mesh=mesh,
        in_specs=placed,
        out_specs=(P("col", "row"), P("col", "row"), P("row", "col"), P("col", "row")),
        check_vma=False,
    )
```

time: 546 us -> 81.5 us (0.15); the launches traced: 535 us -> 81.3 us
  waiting for transfers between devices: 408 us -> 0 us
  blocking collectives: 77.6 us -> 0 us
  Pallas kernels: 0 us -> 73 us
  matrix products: 24.9 us -> 0 us
  between operations: 14.1 us -> 0.64 us
    reduce_scatter x4 -> x0, waiting for transfers between devices: 295 us -> none  [the longest x1 95.9 us: on_device(): lax.psum_scatter(part_active, 'row', scatter_dimension=0, tiled=True)]
    all_gather x2 -> x0, waiting for transfers between devices: 112 us -> none  [the longest x1 58 us: on_device(): lax.all_gather(active, 'row', axis=0, tiled=True)]
    all_gather x2 -> x0, blocking collectives: 77.6 us -> none  [the longest x1 42.6 us: on_device(): lax.all_gather(inputs, 'col', axis=0, tiled=True)]
    pallas_call x0 -> x1, Pallas kernels: none -> 73 us  [on_device(): pl.pallas_call(kernel, out_shape=(shape((32, 768), BF16), shape((32, 768)...]
    dot_general x6 -> x0, matrix products: 24.9 us -> none  [the longest x4 16.3 us: contract(): lax.dot_general(left, right, (((left_dim,), (right_dim,)), ((), ())), pre...]
  transfers between devices with their start and end apart: 6 -> 0, of which waited for: 6 -> 0; matrix products, arithmetic and copies ran while one was open for 5% -> 0% of each run, Pallas kernels for 0% -> 0%
where the time goes in v1:
time: 81.5 us; the launch traced here: 81.3 us
  Pallas kernels  73 us (90%)
  local copies, waits for them, and re-layouts  7.62 us (9%)
    pallas_call x1, Pallas kernels, on_device(): pl.pallas_call(kernel, out_shape=(shape((32, 768), BF16), shape((32, 768)...  73 us
    unnamed x6, local copies, waits for them, and re-layouts  7.62 us

profile of v1, /device:TPU:1, one launch (start us, length us, event | category | flops | bytes accessed | tf_op | source)
XLA Modules:
  0.0 81.3 jit_solution(4076473212683645059)
XLA Ops:
  0.6 73.0 %shard_map.75 = (bf16[32,768]{1,0:T(8,128)(2,1)}, bf16[32,768]{1,0:T(8,128)(2,1)}, bf16[768,1536]{1,0:T(8,128)(2,1)}, bf16[1536,768]{1,0:T(8,128)(2,1)}) custom-call(bf16[32,768]{1,0:T(8,128)(2,1)} %inputs.1, bf16[768,1536]{1,0:T(8,128)(2,1)} %w_up.1, bf16[1536,768]{1,0:T(8,128)(2,1)} %w_down.1, bf16[32,768]{1,0:T(8,128)(2,1)} %grad_out.1), custom_call_target="tpu_custom_call" | custom-call | tf_op jit(solution)/shard_map/pallas_call | solution.py:237
  73.7 1.4 %copy.12 = bf16[32,768]{1,0:T(8,128)(2,1)} copy(bf16[32,768]{1,0:T(8,128)(2,1)} %get-tuple-element.8) | data formatting | bytes 98304
  75.1 1.4 %copy.13 = bf16[32,768]{1,0:T(8,128)(2,1)} copy(bf16[32,768]{1,0:T(8,128)(2,1)} %get-tuple-element.9) | data formatting | bytes 98304
  76.5 0.0 copy-start
  76.5 3.4 %copy.14 = bf16[768,1536]{1,0:T(8,128)(2,1)} copy(bf16[768,1536]{1,0:T(8,128)(2,1)} %get-tuple-element.10) | data formatting | bytes 4718592
  79.9 0.0 copy-done
  79.9 1.4 %copy.15 = bf16[1536,768]{1,0:T(8,128)(2,1)} copy(bf16[1536,768]{1,0:T(8,128)(2,1)S(1)} %copy-done) | data formatting | bytes 4718592
Async XLA Ops:
  76.5 3.4 %copy-start = (bf16[1536,768]{1,0:T(8,128)(2,1)S(1)}, bf16[1536,768]{1,0:T(8,128)(2,1)}, u32[]{:S(2)}) copy-start(bf16[1536,768]{1,0:T(8,128)(2,1)} %get-tuple-element.11) | copy-start | bytes 7077892

commit v2 on v1

--- a/solution.py
+++ b/solution.py
@@ -10,15 +10,14 @@
 MESH = pl.DeviceIdType.MESH
 BF16, F32 = jnp.bfloat16, jnp.float32
 ORDER = (
-    (0, 1, 0), (1, 0, 0), (0, 1, 1), (1, 0, 1), (2, 0, 0), (0, 2, 0), (0, 2, 1), (1, 1, 0),
-    (2, 0, 1), (0, 3, 0), (1, 1, 1), (2, 1, 0), (0, 3, 1), (3, 0, 0), (1, 2, 0), (2, 1, 1),
-    (1, 2, 1), (3, 0, 1), (2, 2, 0), (1, 3, 0), (3, 1, 0), (2, 2, 1), (4, 0, 0), (1, 3, 1),
-    (3, 1, 1), (2, 3, 0), (4, 0, 1), (3, 2, 0), (2, 3, 1), (4, 1, 0), (3, 2, 1), (5, 0, 0),
-    (4, 1, 1), (3, 3, 0), (5, 0, 1), (3, 3, 1), (4, 2, 0), (5, 1, 0), (6, 0, 0), (4, 2, 1),
-    (5, 1, 1), (7, 0, 0), (6, 0, 1), (4, 3, 0), (4, 3, 1), (6, 1, 0), (5, 2, 0), (7, 0, 1),
-    (5, 2, 1), (7, 1, 0), (6, 1, 1), (8, 0, 0), (5, 3, 0), (7, 1, 1), (6, 2, 0), (5, 3, 1),
-    (8, 0, 1), (6, 2, 1), (7, 2, 0), (8, 1, 0), (7, 2, 1), (6, 3, 0), (8, 1, 1), (6, 3, 1),
-    (7, 3, 0), (7, 3, 1), (8, 2, 0), (8, 2, 1), (8, 3, 0), (8, 3, 1),
+    (1, 0, 0), (0, 3, 0), (2, 0, 0), (0, 3, 1), (0, 2, 0), (0, 2, 1), (0, 1, 0), (1, 3, 0),
+    (0, 1, 1), (0, 0, 1), (3, 0, 0), (1, 3, 1), (2, 3, 0), (1, 2, 0), (2, 3, 1), (1, 2, 1),
+    (2, 2, 0), (1, 1, 0), (4, 0, 0), (3, 3, 0), (2, 2, 1), (1, 1, 1), (3, 3, 1), (2, 1, 0),
+    (1, 0, 1), (3, 2, 0), (2, 1, 1), (2, 0, 1), (6, 0, 0), (4, 3, 0), (3, 2, 1), (7, 0, 0),
+    (4, 3, 1), (3, 1, 0), (4, 2, 0), (3, 1, 1), (3, 0, 1), (4, 2, 1), (8, 0, 0), (6, 3, 0),
+    (4, 1, 0), (7, 3, 0), (6, 3, 1), (4, 1, 1), (6, 2, 0), (4, 0, 1), (7, 3, 1), (6, 2, 1),
+    (7, 2, 0), (6, 1, 0), (7, 2, 1), (8, 3, 0), (6, 1, 1), (7, 1, 0), (7, 1, 1), (8, 3, 1),
+    (6, 0, 1), (8, 2, 0), (7, 0, 1), (8, 2, 1), (8, 1, 0), (8, 1, 1), (8, 0, 1),
 )
 
 
@@ -48,10 +47,10 @@
 
 def kernel(
     inputs, w_up, w_down, grad_out, outputs, grad_in, grad_up, grad_down,
-    tokens, up, down, act, up_out, down_out,
+    tokens, up, down, act,
     core_out, core_in, mine, x_out, x_in, sums, zh_out, zh_in, hidden,
     part, y_out, y_in, kept, z_out, z_in,
-    load_sem, store_sem, own_sem, sent, got,
+    load_sem, own_sem, sent, got,
 ):
     row, col = lax.axis_index("row"), lax.axis_index("col")
     x, zh, core = row // 4, (row // 2) % 2, row % 2
@@ -99,11 +98,13 @@
     def sem(step, q):
         return 8 + 8 * step + q
 
-    for a in range(2):
+    def share(a):
         here = tokens.at[a, at(y * 32, 32)]
         for device in ys:
             send(shards[a], here, device, a, a, 32)
-    for j in (1, 2, 3):
+
+    share(0)
+    for j in (3, 2, 1):
         for a in range(2):
             there = tokens.at[a, at(j * 128 + y * 32, 32)]
             send(shards[a], there, zs[j - 1], sem(0, 2 * j + a), sem(0, 2 * j + a), 32)
@@ -120,8 +121,9 @@
         q = 2 * j + a
         chunk = pl.ds(j * 128, 128)
         group = at(j * 128 + x * 32, 32)
-        piece = at(j * 128 + x * 32 + zh * 16, 16)
-        if step == 0:
+        if step == 0 and j == 0:
+            share(a)
+        elif step == 0:
             shard = tokens.at[a, at(j * 128 + y * 32, 32)]
             arrived(shard, sem(0, q))
             for device in ys:
@@ -129,7 +131,7 @@
         elif step == 1:
             if j == 0:
                 own[a].wait()
-                weights(a)
+            weights(a)
             arrived(tokens.at[a, pl.ds(j * 128, 96)], q)
             block = tokens[a, chunk]
 
@@ -144,32 +146,28 @@
         elif step == 2:
             arrived(core_in.at[q], sem(1, q))
             both = mine[q] + core_in[q]
-            mine[q] = both
             x_out[q] = both.astype(BF16)
             for d in (1, 2, 3):
                 theirs = x_out.at[q, at((x + d) % 4 * 32, 32)]
                 send(theirs, x_in.at[q, d - 1], xs[d - 1], sem(2, q), sem(2, q), 32)
         elif step == 3:
             arrived(x_in.at[q], sem(2, q))
-            total = mine[q, at(x * 32, 32)]
+            rows = at(x * 32, 32)
+            total = mine[q, rows] + core_in[q, rows]
             for d in range(3):
                 total = total + x_in[q, d].astype(F32)
             sums[q] = total
             zh_out[q] = total.astype(BF16)
-            send(zh_out.at[q, at((1 - zh) * 16, 16)], zh_in.at[q], partner, sem(3, q), sem(3, q), 16)
+            send(zh_out.at[q], zh_in.at[q], partner, sem(3, q), sem(3, q), 32)
         elif step == 4:
             arrived(zh_in.at[q], sem(3, q))
-            total = sums[q, at(zh * 16, 16)] + zh_in[q].astype(F32)
+            total = sums[q] + zh_in[q].astype(F32)
             if a == 0:
                 hidden[j] = total
                 result = gelu(total)
             else:
                 result = total * gelu_slope(hidden[j])
-            act[a, core, piece] = result.astype(BF16)
-            theirs = act.at[a, core, piece]
-            send(theirs, theirs, partner, sem(4, q), sem(4, q), 16)
-        elif step == 5:
-            arrived(zh_in.at[q], sem(4, q))
+            act[a, core, group] = result.astype(BF16)
             theirs = act.at[a, core, group]
             for device in xs:
                 send(theirs, theirs, device, sem(5, q), sem(5, q), 32)
@@ -178,6 +176,8 @@
             theirs = act.at[a, core, chunk]
             send(theirs, theirs, other_core, sem(6, q), sem(6, q), 128)
         elif step == 7:
+            weights(1 - a)
+
             def term(half):
                 block = act[a, half, chunk]
                 if a == 0:
@@ -202,15 +202,10 @@
             else:
                 z_out[a, j - 1] = total.astype(BF16)
                 send(z_out.at[a, j - 1], z_in.at[a, j - 1], zs[j - 1], sem(8, a), sem(8, a), 32)
-        if (step, j) == (7, 3):
-            for half in range(2):
-                if a == 0:
-                    down_out[half] = contract(act[0, half], tokens[1], 0, 0).astype(BF16)
-                    src, dst = down_out.at[half], grad_down.at[pl.ds(half * 768, 768)]
-                else:
-                    up_out[half] = contract(tokens[0], act[1, half], 0, 0).astype(BF16)
-                    src, dst = up_out.at[half], grad_up.at[:, pl.ds(half * 768, 768)]
-                pltpu.make_async_copy(src, dst, store_sem.at[a, half]).start()
+
+    for half in range(2):
+        grad_down[pl.ds(half * 768, 768)] = contract(act[0, half], tokens[1], 0, 0).astype(BF16)
+        grad_up[:, pl.ds(half * 768, 768)] = contract(tokens[0], act[1, half], 0, 0).astype(BF16)
 
     for a, result in enumerate((outputs, grad_in)):
         arrived(z_in.at[a], sem(8, a))
@@ -219,36 +214,36 @@
             total = total + z_in[a, j].astype(F32)
         result[...] = total.astype(BF16)
 
-    for half in range(2):
-        pltpu.make_async_copy(
-            down_out.at[half], grad_down.at[pl.ds(half * 768, 768)], store_sem.at[0, half]
-        ).wait()
-        pltpu.make_async_copy(
-            up_out.at[half], grad_up.at[:, pl.ds(half * 768, 768)], store_sem.at[1, half]
-        ).wait()
     for send_sem, rows in flights.items():
         ref = tokens.at[0, pl.ds(0, rows)]
         pltpu.make_async_copy(ref, ref, sent.at[send_sem]).wait()
 
 
+def write(*refs):
+    count = len(refs) // 2
+    sem = refs[-1]
+    copies = [
+        pltpu.make_async_copy(refs[k], refs[count + k], sem.at[k]) for k in range(count)
+    ]
+    for copy in copies:
+        copy.start()
+    for copy in copies:
+        copy.wait()
+
+
 def on_device(inputs, w_up, w_down, grad_out):
-    shape = jax.ShapeDtypeStruct
-    hbm, vmem = pl.BlockSpec(memory_space=pl.ANY), pl.BlockSpec(memory_space=pltpu.VMEM)
-    return pl.pallas_call(
+    shapes = ((32, 768), (32, 768), (768, 1536), (1536, 768))
+    hbm, vmem = pl.BlockSpec(memory_space=pltpu.HBM), pl.BlockSpec(memory_space=pltpu.VMEM)
+    results = pl.pallas_call(
         kernel,
-        out_shape=(
-            shape((32, 768), BF16), shape((32, 768), BF16),
-            shape((768, 1536), BF16), shape((1536, 768), BF16),
-        ),
+        out_shape=tuple(pltpu.VMEM(shape, BF16) for shape in shapes),
         in_specs=[hbm] * 4,
-        out_specs=(vmem, vmem, hbm, hbm),
+        out_specs=(vmem,) * 4,
         scratch_shapes=[
             pltpu.VMEM((2, 512, 768), BF16),
             pltpu.VMEM((2, 768, 768), BF16),
             pltpu.VMEM((2, 768, 768), BF16),
             pltpu.VMEM((2, 2, 512, 768), BF16),
-            pltpu.VMEM((2, 768, 768), BF16),
-            pltpu.VMEM((2, 768, 768), BF16),
             pltpu.VMEM((8, 128, 768), F32),
             pltpu.VMEM((8, 128, 768), F32),
             pltpu.VMEM((8, 128, 768), F32),
@@ -256,15 +251,14 @@
             pltpu.VMEM((8, 3, 32, 768), BF16),
             pltpu.VMEM((8, 32, 768), F32),
             pltpu.VMEM((8, 32, 768), BF16),
-            pltpu.VMEM((8, 16, 768), BF16),
-            pltpu.VMEM((4, 16, 768), F32),
+            pltpu.VMEM((8, 32, 768), BF16),
+            pltpu.VMEM((4, 32, 768), F32),
             pltpu.VMEM((8, 128, 768), F32),
             pltpu.VMEM((8, 128, 768), BF16),
             pltpu.VMEM((8, 3, 32, 768), BF16),
             pltpu.VMEM((2, 32, 768), F32),
             pltpu.VMEM((2, 3, 32, 768), BF16),
             pltpu.VMEM((2, 3, 32, 768), BF16),
-            pltpu.SemaphoreType.DMA((2, 2)),
             pltpu.SemaphoreType.DMA((2, 2)),
             pltpu.SemaphoreType.DMA((2,)),
             pltpu.SemaphoreType.DMA((80,)),
@@ -274,6 +268,14 @@
             collective_id=0, has_side_effects=True, vmem_limit_bytes=56 << 20
         ),
     )(inputs, w_up, w_down, grad_out)
+    return pl.pallas_call(
+        write,
+        out_shape=tuple(jax.ShapeDtypeStruct(shape, BF16) for shape in shapes),
+        in_specs=[pl.BlockSpec(memory_space=pl.ANY)] * 4,
+        out_specs=(hbm,) * 4,
+        scratch_shapes=[pltpu.SemaphoreType.DMA((4,))],
+        compiler_params=pltpu.CompilerParams(vmem_limit_bytes=1 << 20),
+    )(*results)
 
 
 def solution(mesh):

time: 81.5 us -> 75.4 us (0.925)
  local copies, waits for them, and re-layouts: 7.62 us -> 0 us
  Pallas kernels: 73 us -> 74.7 us
    unnamed x6 -> x0, local copies, waits for them, and re-layouts: 7.62 us -> none
    pallas_call x1 -> x2, Pallas kernels: 73 us -> 74.7 us  [the longest x1 72.5 us: on_device(): pl.pallas_call(kernel, out_shape=tuple((pltpu.VMEM(shape, BF16) for shape...]
where the time goes in v2:
time: 75.4 us
  Pallas kernels  74.7 us (99%)
    pallas_call x1, Pallas kernels, on_device(): pl.pallas_call(kernel, out_shape=tuple((pltpu.VMEM(shape, BF16) for shape...  72.5 us
    pallas_call x1, Pallas kernels, on_device(): pl.pallas_call(write, out_shape=tuple((jax.ShapeDtypeStruct(shape, BF16)...  2.25 us

profile of v2, /device:TPU:1, one launch (start us, length us, event | category | flops | bytes accessed | tf_op | source)
XLA Modules:
  0.0 75.4 jit_solution(10983387774903382628)
XLA Ops:
  0.6 72.5 %shard_map.75 = (bf16[32,768]{1,0:T(8,128)(2,1)S(1)}, bf16[32,768]{1,0:T(8,128)(2,1)S(1)}, bf16[768,1536]{1,0:T(8,128)(2,1)S(1)}, bf16[1536,768]{1,0:T(8,128)(2,1)S(1)}) custom-call(bf16[32,768]{1,0:T(8,128)(2,1)} %inputs.1, bf16[768,1536]{1,0:T(8,128)(2,1)} %w_up.1, bf16[1536,768]{1,0:T(8,128)(2,1)} %w_down.1, bf16[32,768]{1,0:T(8,128)(2,1)} %grad_out.1), custom_call_target="tpu_custom_call" | custom-call | tf_op jit(solution)/shard_map/pallas_call | solution.py:237
  73.1 2.3 %shard_map.76 = (bf16[32,768]{1,0:T(8,128)(2,1)}, bf16[32,768]{1,0:T(8,128)(2,1)}, bf16[768,1536]{1,0:T(8,128)(2,1)}, bf16[1536,768]{1,0:T(8,128)(2,1)}) custom-call(bf16[32,768]{1,0:T(8,128)(2,1)S(1)} %get-tuple-element.8.refs_0_, bf16[32,768]{1,0:T(8,128)(2,1)S(1)} %get-tuple-element.9.refs_1_, bf16[768,1536]{1,0:T(8,128)(2,1)S(1)} %get-tuple-element.10.refs_2_, ...), custom_call_target="tpu_custom_call" | custom-call | tf_op jit(solution)/shard_map/pallas_call | solution.py:271

commit v3 on v2

--- a/solution.py
+++ b/solution.py
@@ -10,14 +10,14 @@
 MESH = pl.DeviceIdType.MESH
 BF16, F32 = jnp.bfloat16, jnp.float32
 ORDER = (
-    (1, 0, 0), (0, 3, 0), (2, 0, 0), (0, 3, 1), (0, 2, 0), (0, 2, 1), (0, 1, 0), (1, 3, 0),
-    (0, 1, 1), (0, 0, 1), (3, 0, 0), (1, 3, 1), (2, 3, 0), (1, 2, 0), (2, 3, 1), (1, 2, 1),
-    (2, 2, 0), (1, 1, 0), (4, 0, 0), (3, 3, 0), (2, 2, 1), (1, 1, 1), (3, 3, 1), (2, 1, 0),
-    (1, 0, 1), (3, 2, 0), (2, 1, 1), (2, 0, 1), (6, 0, 0), (4, 3, 0), (3, 2, 1), (7, 0, 0),
-    (4, 3, 1), (3, 1, 0), (4, 2, 0), (3, 1, 1), (3, 0, 1), (4, 2, 1), (8, 0, 0), (6, 3, 0),
-    (4, 1, 0), (7, 3, 0), (6, 3, 1), (4, 1, 1), (6, 2, 0), (4, 0, 1), (7, 3, 1), (6, 2, 1),
-    (7, 2, 0), (6, 1, 0), (7, 2, 1), (8, 3, 0), (6, 1, 1), (7, 1, 0), (7, 1, 1), (8, 3, 1),
-    (6, 0, 1), (8, 2, 0), (7, 0, 1), (8, 2, 1), (8, 1, 0), (8, 1, 1), (8, 0, 1),
+    (0, 0, 1), (0, 1, 0), (1, 0, 0), (0, 2, 0), (1, 0, 1), (0, 3, 0), (2, 0, 0), (1, 1, 0),
+    (0, 3, 1), (2, 0, 1), (1, 2, 0), (0, 2, 1), (2, 1, 0), (0, 1, 1), (1, 3, 0), (2, 2, 0),
+    (1, 3, 1), (3, 0, 0), (2, 3, 0), (1, 2, 1), (3, 1, 0), (2, 3, 1), (1, 1, 1), (3, 2, 0),
+    (2, 2, 1), (3, 3, 0), (2, 1, 1), (3, 3, 1), (4, 1, 0), (3, 2, 1), (4, 2, 0), (3, 1, 1),
+    (4, 3, 0), (3, 0, 1), (4, 3, 1), (6, 1, 0), (4, 2, 1), (6, 2, 0), (7, 1, 0), (4, 1, 1),
+    (6, 3, 0), (4, 0, 0), (7, 2, 0), (6, 3, 1), (7, 3, 0), (4, 0, 1), (6, 2, 1), (7, 3, 1),
+    (6, 1, 1), (8, 1, 0), (7, 2, 1), (8, 2, 0), (6, 0, 0), (7, 1, 1), (8, 3, 0), (6, 0, 1),
+    (7, 0, 0), (8, 3, 1), (7, 0, 1), (8, 2, 1), (8, 1, 1), (8, 0, 0), (8, 0, 1),
 )
 
 
@@ -104,10 +104,9 @@
             send(shards[a], here, device, a, a, 32)
 
     share(0)
-    for j in (3, 2, 1):
-        for a in range(2):
-            there = tokens.at[a, at(j * 128 + y * 32, 32)]
-            send(shards[a], there, zs[j - 1], sem(0, 2 * j + a), sem(0, 2 * j + a), 32)
+    for j, a in ((1, 0), (2, 0), (3, 0), (3, 1), (2, 1), (1, 1)):
+        there = tokens.at[a, at(j * 128 + y * 32, 32)]
+        send(shards[a], there, zs[j - 1], sem(0, 2 * j + a), sem(0, 2 * j + a), 32)
 
     weights_here = set()
 

time: 75.4 us -> 71.8 us (0.952)
  Pallas kernels: 74.7 us -> 71.1 us
    pallas_call x1, Pallas kernels: 72.5 us -> 68.8 us  [on_device(): pl.pallas_call(kernel, out_shape=tuple((pltpu.VMEM(shape, BF16) for shape...]
where the time goes in v3:
time: 71.8 us; the launch traced here: 71.7 us
  Pallas kernels  71.1 us (99%)
    pallas_call x1, Pallas kernels, on_device(): pl.pallas_call(kernel, out_shape=tuple((pltpu.VMEM(shape, BF16) for shape...  68.8 us
    pallas_call x1, Pallas kernels, on_device(): pl.pallas_call(write, out_shape=tuple((jax.ShapeDtypeStruct(shape, BF16)...  2.25 us

profile of v3, /device:TPU:1, one launch (start us, length us, event | category | flops | bytes accessed | tf_op | source)
XLA Modules:
  0.0 71.7 jit_solution(15614372368460105768)
XLA Ops:
  0.6 68.8 %shard_map.75 = (bf16[32,768]{1,0:T(8,128)(2,1)S(1)}, bf16[32,768]{1,0:T(8,128)(2,1)S(1)}, bf16[768,1536]{1,0:T(8,128)(2,1)S(1)}, bf16[1536,768]{1,0:T(8,128)(2,1)S(1)}) custom-call(bf16[32,768]{1,0:T(8,128)(2,1)} %inputs.1, bf16[768,1536]{1,0:T(8,128)(2,1)} %w_up.1, bf16[1536,768]{1,0:T(8,128)(2,1)} %w_down.1, bf16[32,768]{1,0:T(8,128)(2,1)} %grad_out.1), custom_call_target="tpu_custom_call" | custom-call | tf_op jit(solution)/shard_map/pallas_call | solution.py:236
  69.5 2.3 %shard_map.76 = (bf16[32,768]{1,0:T(8,128)(2,1)}, bf16[32,768]{1,0:T(8,128)(2,1)}, bf16[768,1536]{1,0:T(8,128)(2,1)}, bf16[1536,768]{1,0:T(8,128)(2,1)}) custom-call(bf16[32,768]{1,0:T(8,128)(2,1)S(1)} %get-tuple-element.8.refs_0_, bf16[32,768]{1,0:T(8,128)(2,1)S(1)} %get-tuple-element.9.refs_1_, bf16[768,1536]{1,0:T(8,128)(2,1)S(1)} %get-tuple-element.10.refs_2_, ...), custom_call_target="tpu_custom_call" | custom-call | tf_op jit(solution)/shard_map/pallas_call | solution.py:270

commit v4 on v3

--- a/solution.py
+++ b/solution.py
@@ -10,14 +10,15 @@
 MESH = pl.DeviceIdType.MESH
 BF16, F32 = jnp.bfloat16, jnp.float32
 ORDER = (
-    (0, 0, 1), (0, 1, 0), (1, 0, 0), (0, 2, 0), (1, 0, 1), (0, 3, 0), (2, 0, 0), (1, 1, 0),
-    (0, 3, 1), (2, 0, 1), (1, 2, 0), (0, 2, 1), (2, 1, 0), (0, 1, 1), (1, 3, 0), (2, 2, 0),
-    (1, 3, 1), (3, 0, 0), (2, 3, 0), (1, 2, 1), (3, 1, 0), (2, 3, 1), (1, 1, 1), (3, 2, 0),
-    (2, 2, 1), (3, 3, 0), (2, 1, 1), (3, 3, 1), (4, 1, 0), (3, 2, 1), (4, 2, 0), (3, 1, 1),
-    (4, 3, 0), (3, 0, 1), (4, 3, 1), (6, 1, 0), (4, 2, 1), (6, 2, 0), (7, 1, 0), (4, 1, 1),
-    (6, 3, 0), (4, 0, 0), (7, 2, 0), (6, 3, 1), (7, 3, 0), (4, 0, 1), (6, 2, 1), (7, 3, 1),
-    (6, 1, 1), (8, 1, 0), (7, 2, 1), (8, 2, 0), (6, 0, 0), (7, 1, 1), (8, 3, 0), (6, 0, 1),
-    (7, 0, 0), (8, 3, 1), (7, 0, 1), (8, 2, 1), (8, 1, 1), (8, 0, 0), (8, 0, 1),
+    (0, 0, 1), (0, 1, 0), (1, 0, 0), (0, 1, 1), (1, 0, 1), (2, 0, 0), (0, 3, 0), (1, 1, 0),
+    (0, 2, 0), (2, 0, 1), (1, 1, 1), (0, 3, 1), (2, 1, 0), (1, 3, 0), (0, 2, 1), (2, 1, 1),
+    (1, 2, 0), (3, 0, 1), (2, 3, 0), (1, 3, 1), (3, 1, 0), (2, 2, 0), (1, 2, 1), (3, 1, 1),
+    (2, 3, 1), (3, 3, 0), (2, 2, 1), (3, 2, 0), (4, 1, 0), (3, 3, 1), (4, 1, 1), (3, 2, 1),
+    (4, 3, 0), (4, 2, 0), (6, 1, 0), (3, 0, 0), (4, 3, 1), (6, 1, 1), (7, 1, 0), (4, 2, 1),
+    (6, 3, 0), (7, 1, 1), (6, 2, 0), (4, 0, 0), (7, 3, 0), (6, 3, 1), (7, 2, 0), (4, 0, 1),
+    (6, 2, 1), (7, 3, 1), (8, 1, 1), (6, 0, 0), (8, 3, 0), (7, 2, 1), (8, 2, 0), (6, 0, 1),
+    (7, 0, 0), (8, 3, 1), (8, 1, 0), (7, 0, 1), (8, 2, 1), (9, 0, 0), (9, 1, 0), (9, 1, 1),
+    (9, 0, 1), (8, 0, 0), (8, 0, 1),
 )
 
 
@@ -83,6 +84,8 @@
         pl.semaphore_signal(barrier, inc=1, device_id=device, device_id_type=MESH)
     pl.semaphore_wait(barrier, len(everyone))
 
+    for copy in own:
+        copy.wait()
     flights = {}
 
     def send(src, dst, device, send_sem, recv_sem, rows):
@@ -101,12 +104,12 @@
     def share(a):
         here = tokens.at[a, at(y * 32, 32)]
         for device in ys:
-            send(shards[a], here, device, a, a, 32)
+            send(here, here, device, a, a, 32)
 
     share(0)
-    for j, a in ((1, 0), (2, 0), (3, 0), (3, 1), (2, 1), (1, 1)):
+    for j, a in ((1, 0), (3, 0), (1, 1), (3, 1), (2, 0), (2, 1)):
         there = tokens.at[a, at(j * 128 + y * 32, 32)]
-        send(shards[a], there, zs[j - 1], sem(0, 2 * j + a), sem(0, 2 * j + a), 32)
+        send(tokens.at[a, at(y * 32, 32)], there, zs[j - 1], sem(0, 2 * j + a), sem(0, 2 * j + a), 32)
 
     weights_here = set()
 
@@ -128,8 +131,6 @@
             for device in ys:
                 send(shard, shard, device, q, q, 32)
         elif step == 1:
-            if j == 0:
-                own[a].wait()
             weights(a)
             arrived(tokens.at[a, pl.ds(j * 128, 96)], q)
             block = tokens[a, chunk]
@@ -191,7 +192,7 @@
             for d in (1, 2, 3):
                 theirs = y_out.at[q, at((y + d) % 4 * 32, 32)]
                 send(theirs, y_in.at[q, d - 1], ys[d - 1], sem(7, q), sem(7, q), 32)
-        else:
+        elif step == 8:
             arrived(y_in.at[q], sem(7, q))
             total = part[q, at(y * 32, 32)]
             for d in range(3):
@@ -201,10 +202,14 @@
             else:
                 z_out[a, j - 1] = total.astype(BF16)
                 send(z_out.at[a, j - 1], z_in.at[a, j - 1], zs[j - 1], sem(8, a), sem(8, a), 32)
-
-    for half in range(2):
-        grad_down[pl.ds(half * 768, 768)] = contract(act[0, half], tokens[1], 0, 0).astype(BF16)
-        grad_up[:, pl.ds(half * 768, 768)] = contract(tokens[0], act[1, half], 0, 0).astype(BF16)
+        else:
+            half = 1 - core if j else core
+            if a == 0:
+                product = contract(act[0, half], tokens[1], 0, 0)
+                grad_down[at(half * 768, 768)] = product.astype(BF16)
+            else:
+                product = contract(tokens[0], act[1, half], 0, 0)
+                grad_up[:, at(half * 768, 768)] = product.astype(BF16)
 
     for a, result in enumerate((outputs, grad_in)):
         arrived(z_in.at[a], sem(8, a))

time: 71.8 us -> 68.7 us (0.957)
  Pallas kernels: 71.1 us -> 68 us
    pallas_call x1, Pallas kernels: 68.8 us -> 65.7 us  [on_device(): pl.pallas_call(kernel, out_shape=tuple((pltpu.VMEM(shape, BF16) for shape...]
where the time goes in v4:
time: 68.7 us; the launch traced here: 68.6 us
  Pallas kernels  68 us (99%)
    pallas_call x1, Pallas kernels, on_device(): pl.pallas_call(kernel, out_shape=tuple((pltpu.VMEM(shape, BF16) for shape...  65.7 us
    pallas_call x1, Pallas kernels, on_device(): pl.pallas_call(write, out_shape=tuple((jax.ShapeDtypeStruct(shape, BF16)...  2.25 us

profile of v4, /device:TPU:1, one launch (start us, length us, event | category | flops | bytes accessed | tf_op | source)
XLA Modules:
  0.0 68.6 jit_solution(5784212833125505150)
XLA Ops:
  0.6 65.7 %shard_map.75 = (bf16[32,768]{1,0:T(8,128)(2,1)S(1)}, bf16[32,768]{1,0:T(8,128)(2,1)S(1)}, bf16[768,1536]{1,0:T(8,128)(2,1)S(1)}, bf16[1536,768]{1,0:T(8,128)(2,1)S(1)}) custom-call(bf16[32,768]{1,0:T(8,128)(2,1)} %inputs.1, bf16[768,1536]{1,0:T(8,128)(2,1)} %w_up.1, bf16[1536,768]{1,0:T(8,128)(2,1)} %w_down.1, bf16[32,768]{1,0:T(8,128)(2,1)} %grad_out.1), custom_call_target="tpu_custom_call" | custom-call | tf_op jit(solution)/shard_map/pallas_call | solution.py:241
  66.4 2.3 %shard_map.76 = (bf16[32,768]{1,0:T(8,128)(2,1)}, bf16[32,768]{1,0:T(8,128)(2,1)}, bf16[768,1536]{1,0:T(8,128)(2,1)}, bf16[1536,768]{1,0:T(8,128)(2,1)}) custom-call(bf16[32,768]{1,0:T(8,128)(2,1)S(1)} %get-tuple-element.8.refs_0_, bf16[32,768]{1,0:T(8,128)(2,1)S(1)} %get-tuple-element.9.refs_1_, bf16[768,1536]{1,0:T(8,128)(2,1)S(1)} %get-tuple-element.10.refs_2_, ...), custom_call_target="tpu_custom_call" | custom-call | tf_op jit(solution)/shard_map/pallas_call | solution.py:275

commit v5 on v4

--- a/solution.py
+++ b/solution.py
@@ -64,6 +64,11 @@
     zs = [(row, plane * 4 + y) for plane in planes[1:]]
     shards = (inputs, grad_out)
 
+    barrier = pltpu.get_barrier_semaphore()
+    everyone = [other_core, partner] + xs + ys + zs
+    for device in everyone:
+        pl.semaphore_signal(barrier, inc=1, device_id=device, device_id_type=MESH)
+
     loads = []
     for half in range(2):
         for k, (src, dst) in enumerate((
@@ -78,10 +83,6 @@
     for copy in own + loads:
         copy.start()
 
-    barrier = pltpu.get_barrier_semaphore()
-    everyone = [other_core, partner] + xs + ys + zs
-    for device in everyone:
-        pl.semaphore_signal(barrier, inc=1, device_id=device, device_id_type=MESH)
     pl.semaphore_wait(barrier, len(everyone))
 
     for copy in own:
@@ -147,7 +148,7 @@
             arrived(core_in.at[q], sem(1, q))
             both = mine[q] + core_in[q]
             x_out[q] = both.astype(BF16)
-            for d in (1, 2, 3):
+            for d in (2, 1, 3):
                 theirs = x_out.at[q, at((x + d) % 4 * 32, 32)]
                 send(theirs, x_in.at[q, d - 1], xs[d - 1], sem(2, q), sem(2, q), 32)
         elif step == 3:
@@ -189,7 +190,7 @@
             total = total + term(1 - core)
             part[q] = total
             y_out[q] = total.astype(BF16)
-            for d in (1, 2, 3):
+            for d in (2, 1, 3):
                 theirs = y_out.at[q, at((y + d) % 4 * 32, 32)]
                 send(theirs, y_in.at[q, d - 1], ys[d - 1], sem(7, q), sem(7, q), 32)
         elif step == 8:

time: 68.7 us -> 68 us (0.990)
  Pallas kernels: 68 us -> 67.3 us
    pallas_call x1, Pallas kernels: 65.7 us -> 65 us  [on_device(): pl.pallas_call(kernel, out_shape=tuple((pltpu.VMEM(shape, BF16) for shape...]
where the time goes in v5:
time: 68 us; the launch traced here: 67.9 us
  Pallas kernels  67.3 us (99%)
    pallas_call x1, Pallas kernels, on_device(): pl.pallas_call(kernel, out_shape=tuple((pltpu.VMEM(shape, BF16) for shape...  65 us
    pallas_call x1, Pallas kernels, on_device(): pl.pallas_call(write, out_shape=tuple((jax.ShapeDtypeStruct(shape, BF16)...  2.25 us

profile of v5, /device:TPU:1, one launch (start us, length us, event | category | flops | bytes accessed | tf_op | source)
XLA Modules:
  0.0 67.9 jit_solution(17688014201495999081)
XLA Ops:
  0.6 65.0 %shard_map.75 = (bf16[32,768]{1,0:T(8,128)(2,1)S(1)}, bf16[32,768]{1,0:T(8,128)(2,1)S(1)}, bf16[768,1536]{1,0:T(8,128)(2,1)S(1)}, bf16[1536,768]{1,0:T(8,128)(2,1)S(1)}) custom-call(bf16[32,768]{1,0:T(8,128)(2,1)} %inputs.1, bf16[768,1536]{1,0:T(8,128)(2,1)} %w_up.1, bf16[1536,768]{1,0:T(8,128)(2,1)} %w_down.1, bf16[32,768]{1,0:T(8,128)(2,1)} %grad_out.1), custom_call_target="tpu_custom_call" | custom-call | tf_op jit(solution)/shard_map/pallas_call | solution.py:242
  65.7 2.3 %shard_map.76 = (bf16[32,768]{1,0:T(8,128)(2,1)}, bf16[32,768]{1,0:T(8,128)(2,1)}, bf16[768,1536]{1,0:T(8,128)(2,1)}, bf16[1536,768]{1,0:T(8,128)(2,1)}) custom-call(bf16[32,768]{1,0:T(8,128)(2,1)S(1)} %get-tuple-element.8.refs_0_, bf16[32,768]{1,0:T(8,128)(2,1)S(1)} %get-tuple-element.9.refs_1_, bf16[768,1536]{1,0:T(8,128)(2,1)S(1)} %get-tuple-element.10.refs_2_, ...), custom_call_target="tpu_custom_call" | custom-call | tf_op jit(solution)/shard_map/pallas_call | solution.py:276
